TPU v7x, 32 devices: a whole 2x2x4 slice. The times are simulated.
32 devices in a mesh: groups: 2 (over x), expert: 16 (over z, y, core).
Axes of the slice: x: 2, y: 2, z: 4, core: 2. Of those that a mesh axis runs over, the one named last changes fastest.
Arguments:
- tokens: bfloat16 [4096, 3584], P(('groups', 'expert')), parts along dimension 0, may hold values from -6 to 6
- expert_ids: int32 [4096, 8], P(('groups', 'expert')), parts along dimension 0, may hold values from 0 to 255, all different within a row
- lengths: int32 [2], P('groups'), parts along dimension 0, may hold values from 1024 to 2048
- router: bfloat16 [256, 3584], P('expert'), may hold values from -0.09375 to 0.09375
- w_gate: bfloat16 [16, 3584, 512], P('expert'), may hold values from -0.09375 to 0.09375
- w_up: bfloat16 [16, 3584, 512], P('expert'), may hold values from -0.09375 to 0.09375
- w_down: bfloat16 [16, 512, 3584], P('expert'), may hold values from -0.125 to 0.125
Outputs:
- mixed: bfloat16 [4096, 3584], P(('groups', 'expert')), parts along dimension 0
There are 2 independent parts, one for each index of `groups`. A program takes and returns all parts, laid end to end along the dimension named above; an argument that names none is the same for every part. Nothing has to cross between parts.
Inputs may be any that keep to these rules, and one draw needn't show every extreme that they name: `expert_ids`: each row names 8 different experts.
All inputs are finite; a program needn't handle non-finite values.
Results may differ from a plain program's by a relative error of at most 0.0057.
Values may be sent and summed in bfloat16 or wider, within the bound.
A program may use at most 64 MiB of HBM per device.

v0:
```python
import jax
import jax.numpy as jnp
from jax import lax
from jax.sharding import PartitionSpec as P

SPLIT = 4
SEQ_LEN = 2048
CAP = 4


def shards(tokens, expert_ids, lengths, router, w_gate, w_up, w_down):
    n_dev = lax.axis_size("expert")
    window = n_dev // SPLIT
    tok_rows = tokens.shape[0]
    routes_per = expert_ids.shape[1]
    width = tokens.shape[1]
    product = lax.dot_general(
        tokens,
        lax.all_gather(router, "expert", axis=0, tiled=True),
        (((1,), (1,)), ((), ())),
        preferred_element_type=jnp.float32,
    )
    scores = jax.nn.sigmoid(product)
    picked = jnp.take_along_axis(scores, expert_ids, axis=1)
    route_gate = 2.5 * picked / jnp.sum(picked, axis=1, keepdims=True)
    my_index = lax.axis_index("expert")
    position = my_index * tok_rows + jnp.arange(tok_rows, dtype=jnp.int32)
    sequence = position // SEQ_LEN
    seq_table = (
        sequence[:, None] == jnp.arange(lengths.shape[0], dtype=jnp.int32)[None, :]
    ).astype(jnp.int32)
    length_of = jnp.sum(seq_table * lengths[None, :], axis=1)
    is_live = position % SEQ_LEN < length_of
    flat_ids = expert_ids.reshape(tok_rows * routes_per)
    live_routes = jnp.repeat(is_live, routes_per)
    in_window = (
        (flat_ids[:, None] == jnp.arange(window, dtype=jnp.int32)[None, :]) & live_routes[:, None]
    ).astype(jnp.int32)
    slot_index = jnp.cumsum(in_window, axis=0) - in_window
    kept_route = in_window * (slot_index < CAP).astype(jnp.int32)
    slot_onehot = kept_route[..., None] * (
        slot_index[..., None] == jnp.arange(CAP, dtype=jnp.int32)
    ).astype(jnp.int32)
    slot_onehot = slot_onehot.reshape(tok_rows, routes_per, window, CAP).astype(jnp.float32)
    dispatch = jnp.sum(slot_onehot, axis=1).astype(jnp.bfloat16)
    combine = jnp.einsum("tkwc,tk->wct", slot_onehot, route_gate, precision=lax.Precision.HIGHEST)
    dispatched = jnp.einsum(
        "twc,td->wcd", dispatch, tokens, preferred_element_type=jnp.float32
    ).astype(jnp.bfloat16)
    outgoing = jnp.repeat(dispatched, SPLIT, axis=0)
    received = lax.all_to_all(outgoing, "expert", split_axis=0, concat_axis=0, tiled=True)
    sources, slots, features = received.shape
    flat_rows = received.reshape(sources * slots, features)
    gate_act = jnp.dot(flat_rows, w_gate[0], preferred_element_type=jnp.float32)
    up_act = jnp.dot(flat_rows, w_up[0], preferred_element_type=jnp.float32)
    hidden = (jax.nn.silu(gate_act) * up_act).astype(jnp.bfloat16)
    partial_value = jnp.dot(hidden, w_down[0], preferred_element_type=jnp.float32).astype(
        jnp.bfloat16
    )
    partials = partial_value.reshape(sources, slots, features)
    returned = lax.all_to_all(partials, "expert", split_axis=0, concat_axis=0, tiled=True)
    expert_out = jnp.sum(returned.reshape(window, SPLIT, CAP, width).astype(jnp.float32), axis=1)
    mixed = jnp.einsum("wct,wcd->td", combine, expert_out, precision=lax.Precision.HIGHEST)
    return mixed.astype(jnp.bfloat16)


def solution(mesh):
    placed = (
        P(("groups", "expert"), None),
        P(("groups", "expert"), None),
        P("groups"),
        P("expert", None),
        P("expert", None, None),
        P("expert", None, None),
        P("expert", None, None),
    )
    return jax.shard_map(
        shards, mesh=mesh, in_specs=placed, out_specs=P(("groups", "expert"), None), check_vma=False
    )
```

profile of v0, /device:TPU:0, one launch (start us, length us, event | category | flops | bytes accessed | tf_op | source)
XLA Modules:
  0.0 115.1 jit_solution(11822403496533072971)
XLA Ops:
  6.5 0.0 copy-start
  6.5 0.0 all-gather.2.cloned.1.call-start
  6.5 0.7 all-gather.2.cloned.1.call-update
  7.3 0.8 copy.41
  8.1 0.1 eq.53
  8.1 0.1 eq.58
  8.2 0.7 bitcast_or_fusion
  8.9 0.1 copy.39
  9.0 0.1 reshape.68
  9.8 0.1 broadcast_in_dim.22
  9.9 0.1 broadcast_in_dim.23
  10.0 1.1 reduce-window.6
  11.2 0.2 slice_reduce_fusion
  11.4 0.2 reduce-window.9
  11.6 0.1 broadcast_in_dim.24
  11.7 0.1 and.50
  11.8 0.1 add_bitcast_fusion
  11.9 0.2 mul.52
  12.0 0.1 copy.44
  12.1 0.2 eq.63
  12.3 0.1 copy.43
  12.4 40.6 %all-gather.2.cloned.1.call-done = bf16[256,3584]{1,0:T(8,128)(2,1)} async-done(((bf16[16,3584]{1,0:T(8,128)(2,1)}), bf16[256,3584]{1,0:T(8,128)(2,1)}) %all-gather.2.cloned.1.call-update) | async-done | bytes 1835024 | tf_op jit(solution)/shard_map/all_gather | solution.py:19
  53.0 0.0 copy-done
  53.0 2.2 %fusion.8 = f32[128,256]{1,0:T(8,128)S(1)} fusion(bf16[128,3584]{1,0:T(8,128)(2,1)S(1)} %copy-done, bf16[256,3584]{1,0:T(8,128)(2,1)} %all-gather.2.cloned.1.call-done), kind=kOutput, calls=%fused_computation.13 | convolution fusion | flops 234979328 | bytes 2883584 | tf_op jit(solution)/shard_map/dot_general | solution.py:17
  55.3 0.0 copy-start.1
  55.3 8.6 %gather_fusion = f32[1024]{0:T(1024)S(1)} fusion(f32[128,256]{1,0:T(8,128)S(1)} %fusion.8, s32[1024]{0:T(1024)S(1)} %reshape.68), kind=kCustom, calls=%fused_computation | custom fusion | bytes 16384 | tf_op jit(solution)/shard_map/jit(take_along_axis)/gather | solution.py:24
  63.9 0.1 reshape.71
  64.0 0.0 copy-done.1
  64.1 0.1 multiply_reduce_fusion
  64.1 0.2 convolution_convert_fusion.1
  64.4 0.1 broadcast_in_dim.25
  64.5 16.4 %all_to_all.10 = bf16[16,4,3584]{2,1,0:T(4,128)(2,1)S(1)} all-to-all(bf16[16,4,3584]{2,1,0:T(4,128)(2,1)S(1)} %bitcast.60), channel_id=1, replica_groups=mesh['groups'=2,'expert'=16] {'expert'}, dimensions={0} | all-to-all | bytes 917504 | tf_op jit(solution)/shard_map/all_to_all | solution.py:51
  80.9 0.1 reshape.65
  81.0 2.8 %fusion.4 = f32[64,512]{1,0:T(8,128)S(1)} fusion(bf16[64,3584]{1,0:T(8,128)(2,1)S(1)} %reshape.65, bf16[1,3584,512]{2,1,0:T(8,128)(2,1)} %param.11), kind=kOutput, calls=%fused_computation.8 | convolution fusion | flops 234881024 | bytes 4259840 | tf_op jit(solution)/shard_map/dot_general | solution.py:54
  83.8 4.6 %convolution_convert_fusion = bf16[64,3584]{1,0:T(8,128)(2,1)S(1)} fusion(bf16[1,512,3584]{2,1,0:T(8,128)(2,1)} %param.13, bf16[64,3584]{1,0:T(8,128)(2,1)S(1)} %reshape.65, bf16[1,3584,512]{2,1,0:T(8,128)(2,1)} %param.12, f32[64,512]{1,0:T(8,128)S(1)} %fusion.4), kind=kOutput, calls=%fused_computation.3 | convolution fusion | flops 470188032 | bytes 8388608 | tf_op jit(solution)/shard_map/dot_general | solution.py:57
  88.4 0.1 reshape.66
  88.5 16.9 %all_to_all.11 = bf16[16,4,3584]{2,1,0:T(4,128)(2,1)S(1)} all-to-all(bf16[16,4,3584]{2,1,0:T(4,128)(2,1)S(1)} %reshape.66), channel_id=1, replica_groups=mesh['groups'=2,'expert'=16] {'expert'}, dimensions={0} | all-to-all | bytes 917504 | tf_op jit(solution)/shard_map/all_to_all | solution.py:61
  105.5 0.2 convert_reduce_fusion
  105.7 2.6 %fusion = bf16[128,3584]{1,0:T(8,128)(2,1)} fusion(f32[4,4,3584]{2,1,0:T(4,128)S(1)} %convert_reduce_fusion, f32[128,4,4]{0,2,1:T(4,128)S(1)} %get-tuple-element.5), kind=kOutput, calls=%fused_computation.2 | convolution fusion | flops 88539136 | bytes 1155072 | tf_op jit(solution)/shard_map/wct,wcd->td/dot_general | solution.py:63
  (7 shorter events, 0.2 us)
Async XLA Ops:
  6.5 46.5 %copy-start = (bf16[128,3584]{1,0:T(8,128)(2,1)S(1)}, bf16[128,3584]{1,0:T(8,128)(2,1)}, u32[]{:S(2)}) copy-start(bf16[128,3584]{1,0:T(8,128)(2,1)} %param.7) | copy-start | bytes 2752516
  6.5 46.5 %all-gather.2.cloned.1.call-start = ((), (), s32[]{:S(2)}) async-start(), calls=%async_computation.2 | async-start | bytes 1949696 | tf_op jit(solution)/shard_map/all_gather | solution.py:19
  55.3 8.7 %copy-start.1 = (s32[128,8]{0,1:T(8,128)S(1)}, s32[128,8]{0,1:T(8,128)}, u32[]{:S(2)}) copy-start(s32[128,8]{0,1:T(8,128)} %param.8) | copy-start | bytes 12292
Sparse Core Ops, SparseCore 0:
  9.6 43.3 all-gather.1
where the time goes:
time: 115 us
  waiting for transfers between devices  41.3 us (36%)
  blocking collectives  33.4 us (29%)
  between operations  14.2 us (12%)
  matrix products  12.4 us (11%)
  local copies, waits for them, and re-layouts  11.3 us (10%)
  other arithmetic  2.48 us (2%)
    all_gather x1, waiting for transfers between devices, shards(): lax.all_gather(router, 'expert', axis=0, tiled=True)  40.6 us
    all_to_all x1, blocking collectives, shards(): lax.all_to_all(partials, 'expert', split_axis=0, concat_axis=0, tiled=True)  16.9 us
    all_to_all x1, blocking collectives, shards(): lax.all_to_all(outgoing, 'expert', split_axis=0, concat_axis=0, tiled=True)  16.4 us
    gather x5, local copies, waits for them, and re-layouts, shards(): picked = jnp.take_along_axis(scores, expert_ids, axis=1)  8.91 us
    dot_general x1, matrix products, shards(): jnp.dot(hidden, w_down[0], preferred_element_type=jnp.float32)  4.62 us
    dot_general x1, matrix products, shards(): gate_act = jnp.dot(flat_rows, w_gate[0], preferred_element_type=jnp.float32)  2.78 us
    dot_general x1, matrix products, shards(): jnp.einsum('wct,wcd->td', combine, expert_out, precision=lax.Precision.HI...  2.59 us
  transfers between devices with their start and end apart: 1, of which 1 were waited for; matrix products, arithmetic and copies ran while one was open for 4% of the time, Pallas kernels for 0%

commit v1 on v0

v1 whole, which is shorter than its diff:
```python
import functools

import jax
import jax.numpy as jnp
from jax import lax
from jax.experimental import pallas as pl
from jax.experimental.pallas import tpu as pltpu
from jax.sharding import PartitionSpec as P

SPLIT = 4
SEQ_LEN = 2048
CAP = 4
FOLD = 16 // CAP
F32, BF16 = jnp.float32, jnp.bfloat16


def mod(a, b):
    return lax.rem(a, jnp.int32(b))


def iota(shape, axis):
    return lax.broadcasted_iota(jnp.int32, shape, axis)


def dot(a, b):
    return jnp.dot(a, b, preferred_element_type=F32)


def dot_nt(a, b):
    return lax.dot_general(a, b, (((1,), (1,)), ((), ())), preferred_element_type=F32)


def kernel(
    n, local, tokens_hbm, ids_hbm, len_hbm, router_hbm, gate_hbm, up_hbm, down_hbm, out_hbm,
    tok, ids, length, wg, wu, wd, routed, fold_out, fold_in, x, hidden, part, reduced, back_out, back,
    logit, logits, mask, num_mask, onehot, out,
    load_sem, out_sem, disp_s, disp_r, rout_s, rout_r, fwd_s, fwd_r, red_s, red_r, back_s, back_r, log_s, log_r,
):
    win = n // SPLIT
    rows = win * 16
    per = win * CAP
    rows_tok, width = tok.shape
    quarter = width // FOLD
    lanes = logit.shape[1]
    epad = routed.shape[1]
    me = lax.axis_index("expert")
    w = lax.div(me, jnp.int32(SPLIT))
    r = me - w * SPLIT

    def other(dw, dr):
        return {"expert": mod(w + (dw + win), win) * SPLIT + mod(r + (dr + SPLIT), SPLIT)}

    loads = [
        pltpu.make_async_copy(src, dst, load_sem.at[i])
        for i, (src, dst) in enumerate(
            [
                (ids_hbm, ids), (len_hbm, length), (tokens_hbm, tok), (router_hbm, routed.at[0]),
                (gate_hbm.at[0], wg), (up_hbm.at[0], wu), (down_hbm.at[0], wd),
            ]
        )
    ]
    for load in loads:
        load.start()

    barrier = pltpu.get_barrier_semaphore()
    for step in range(1, n):
        pl.semaphore_signal(
            barrier, inc=1, device_id={"expert": mod(me + step, n)}, device_id_type=pl.DeviceIdType.MESH
        )

    def send(src, dst, s_sem, r_sem, device):
        copy = pltpu.make_async_remote_copy(
            src_ref=src, dst_ref=dst, send_sem=s_sem, recv_sem=r_sem,
            device_id=device, device_id_type=pl.DeviceIdType.MESH,
        )
        return copy

    loads[0].wait()
    loads[1].wait()
    ids_b = ids[...].astype(F32).astype(BF16)
    eye = (iota((8, 8), 0) == iota((8, 8), 1)).astype(F32).astype(BF16)
    ids_t = dot_nt(eye, ids_b).astype(jnp.int32)
    first = me * rows_tok
    alive = mod(first, SEQ_LEN) + iota((rows, rows_tok), 1) < length[lax.div(first, jnp.int32(SEQ_LEN))]
    row = iota((rows, rows_tok), 0)
    expert = mod(w + lax.div(row, jnp.int32(16)), win)
    chosen = ids_t[0:1, :] == expert
    for k in range(1, ids_t.shape[0]):
        chosen = chosen | (ids_t[k : k + 1, :] == expert)
    inside = jnp.where(chosen & alive, 1.0, 0.0)
    earlier = (iota((rows_tok, rows_tok), 0) < iota((rows_tok, rows_tok), 1)).astype(F32).astype(BF16)
    before = dot(inside.astype(BF16), earlier)
    hot = jnp.where(before == mod(row, CAP).astype(F32), inside, 0.0)
    onehot[...] = hot
    turn = mod(lax.div(row, jnp.int32(CAP)), FOLD)

    loads[2].wait()
    folded = jnp.zeros((rows, quarter), F32)
    for q in range(FOLD):
        picked = jnp.where(turn == q, hot, 0.0).astype(BF16)
        folded = folded + dot(picked, tok[:, q * quarter : (q + 1) * quarter])
    folded = folded.astype(BF16)
    fold_in[0, 0] = folded[:16]
    for dw in range(1, win):
        fold_out[dw] = folded[dw * 16 : (dw + 1) * 16]

    pl.semaphore_wait(barrier, n - 1)
    sends = []
    disp = [None]
    for dw in range(1, win):
        disp.append(send(fold_out.at[dw], fold_in.at[0, dw], disp_s.at[dw], disp_r.at[dw], other(dw, 0)))
        disp[dw].start()
    fwd = {}
    for dr in range(1, SPLIT):
        fwd[0, dr] = send(
            fold_in.at[0, 0], fold_in.at[dr, 0], fwd_s.at[0, dr], fwd_r.at[0, dr], other(0, dr)
        )
        fwd[0, dr].start()
    loads[3].wait()
    rout = [None]
    for dw in range(1, win):
        rout.append(send(routed.at[0], routed.at[dw], rout_s.at[dw], rout_r.at[dw], other(dw, 0)))
        rout[dw].start()

    for dw in range(1, win):
        disp[dw].wait_recv()
        for dr in range(1, SPLIT):
            fwd[dw, dr] = send(
                fold_in.at[0, dw], fold_in.at[dr, dw], fwd_s.at[dw, dr], fwd_r.at[dw, dr], other(0, dr)
            )
            fwd[dw, dr].start()

    slot_ids = dot(hot.astype(BF16), ids_b)
    srow = iota((rows, lanes), 0)
    lane = iota((rows, lanes), 1)
    slot_dw = lax.div(srow, jnp.int32(16))
    lane_dw = lax.div(lane, jnp.int32(epad))
    lane_e = lane - lane_dw * epad
    good = (lane_dw < win) & (lane_e < local)
    mine = mod(w + slot_dw, win)
    for i in range(SPLIT):
        chunk = mod(w + slot_dw - lane_dw + 2 * win, win) * SPLIT + mod(r + i, SPLIT)
        which = jnp.where(good, chunk * local + lane_e, -1)
        as_float = which.astype(F32)
        hit = jnp.zeros((rows, lanes), F32)
        for k in range(ids_b.shape[1]):
            hit = jnp.where(as_float == slot_ids[:, k : k + 1], 1.0, hit)
        mask[i] = hit
        num_mask[i] = jnp.where(which == mine, 1.0, 0.0)

    prow, pcol = iota((rows, rows), 0), iota((rows, rows), 1)
    q_of, dw_of, c_of = lax.div(prow, jnp.int32(per)), lax.div(mod(prow, per), jnp.int32(CAP)), mod(prow, CAP)
    perm = (pcol == dw_of * 16 + q_of * CAP + c_of).astype(F32).astype(BF16)
    for i in range(SPLIT):
        if i:
            for dw in range(win):
                fwd[dw, i].wait_recv()
        plain = dot(perm, fold_in[i].reshape(rows, quarter)).astype(BF16)
        for q in range(FOLD):
            x[i * per : (i + 1) * per, q * quarter : (q + 1) * quarter] = plain[q * per : (q + 1) * per]

    loads[4].wait()
    loads[5].wait()
    units = wg.shape[1]
    half = units // 2
    for piece in range(2):
        cols = slice(piece * half, (piece + 1) * half)
        g = dot(x[...], wg[:, cols])
        u = dot(x[...], wu[:, cols])
        hidden[:, cols] = (g * jax.nn.sigmoid(g) * u).astype(BF16)
    loads[6].wait()
    red = {}
    for q in range(FOLD):
        part[q] = dot(hidden[...], wd[:, q * quarter : (q + 1) * quarter]).astype(BF16).reshape(
            SPLIT, per, quarter
        )
        for i in range(1, SPLIT):
            red[q, i] = send(
                part.at[q, i], reduced.at[q, i], red_s.at[q, i], red_r.at[q, i], other(0, -i)
            )
            red[q, i].start()

    for dw in range(1, win):
        rout[dw].wait_recv()
    logit[...] = jnp.zeros_like(logit)
    logit[:, : win * epad] = dot_nt(x[...], routed[...].reshape(win * epad, width))
    logs = {}
    for i in range(SPLIT):
        for dw in range(win):
            src = logit.at[pl.ds(i * per + dw // 2 * 8, 8)]
            if i or dw:
                logs[i, dw] = send(src, logits.at[i, dw], log_s.at[i, dw], log_r.at[i, dw], other(-dw, -i))
                logs[i, dw].start()
            else:
                logits[0, 0] = logit[:8]

    frow, fcol = iota((rows, per), 0), iota((rows, per), 1)
    place = lax.div(frow, jnp.int32(16)) * CAP + mod(frow, CAP)
    total = jnp.zeros((rows, quarter), F32)
    for q in range(FOLD):
        summed = part[q, 0].astype(F32)
        for i in range(1, SPLIT):
            red[q, i].wait_recv()
            summed = summed + reduced[q, i].astype(F32)
        spread = ((fcol == place) & (mod(lax.div(frow, jnp.int32(CAP)), FOLD) == q)).astype(F32).astype(BF16)
        total = total + dot(spread, summed.astype(BF16))
    total = total.astype(BF16)
    back[0] = total[:16]
    backs = [None]
    for dw in range(1, win):
        back_out[dw] = total[dw * 16 : (dw + 1) * 16]
        backs.append(send(back_out.at[dw], back.at[dw], back_s.at[dw], back_r.at[dw], other(-dw, 0)))
        backs[dw].start()

    for pair in logs:
        logs[pair].wait_recv()
    erow, ecol = iota((rows, win * 8), 0), iota((rows, win * 8), 1)
    edw = lax.div(erow, jnp.int32(16))
    expand = jnp.where(ecol == edw * 8 + mod(edw, 2) * CAP + mod(erow, CAP), 1.0, 0.0)
    den = jnp.zeros((rows, 1), F32)
    num = jnp.zeros((rows, 1), F32)
    for i in range(SPLIT):
        spread = jnp.dot(
            expand, logits[i].reshape(win * 8, lanes), preferred_element_type=F32, precision=lax.Precision.HIGHEST
        )
        score = jax.nn.sigmoid(spread)
        den = den + jnp.sum(jnp.where(mask[i] > 0.5, score, 0.0), axis=1, keepdims=True)
        num = num + jnp.sum(jnp.where(num_mask[i] > 0.5, score, 0.0), axis=1, keepdims=True)
    hot = onehot[...]
    filled = jnp.sum(hot, axis=1, keepdims=True) > 0.5
    weight = jnp.where(filled, 2.5 * num / jnp.where(filled, den, 1.0), 0.0)
    combine = (hot * weight).T
    high = combine.astype(BF16).astype(F32)
    middle = (combine - high).astype(BF16).astype(F32)
    low = combine - high - middle
    ccol = mod(lax.div(iota((rows_tok, rows), 1), jnp.int32(CAP)), FOLD)

    for dw in range(1, win):
        backs[dw].wait_recv()
    returned = back[...].reshape(rows, quarter)
    stores = []
    for q in range(FOLD):
        cols = slice(q * quarter, (q + 1) * quarter)
        acc = jnp.zeros((rows_tok, quarter), F32)
        for piece in (high, middle, low):
            acc = acc + dot(jnp.where(ccol == q, piece, 0.0).astype(BF16), returned)
        out[:, cols] = acc.astype(BF16)
        stores.append(pltpu.make_async_copy(out.at[:, cols], out_hbm.at[:, cols], out_sem.at[q]))
        stores[q].start()

    for copies in (disp[1:], rout[1:], backs[1:], fwd.values(), red.values(), logs.values()):
        for copy in copies:
            copy.wait_send()
    for store in stores:
        store.wait()


def shards(tokens, expert_ids, lengths, router, w_gate, w_up, w_down):
    n = lax.axis_size("expert")
    win = n // SPLIT
    rows_tok, width = tokens.shape
    quarter = width // FOLD
    units = w_gate.shape[2]
    local = router.shape[0]
    epad = -(-local // 16) * 16
    if epad != local:
        router = jnp.pad(router, ((0, epad - local), (0, 0)))
    lanes = -(-win * epad // 128) * 128
    rows, per = win * 16, win * CAP
    vmem = pltpu.VMEM
    sems = pltpu.SemaphoreType.DMA
    scratch = [
        vmem((rows_tok, width), BF16),
        vmem(expert_ids.shape, jnp.int32),
        pltpu.SMEM(lengths.shape, jnp.int32),
        vmem((width, units), BF16),
        vmem((width, units), BF16),
        vmem((units, width), BF16),
        vmem((win, epad, width), BF16),
        vmem((win, 16, quarter), BF16),
        vmem((SPLIT, win, 16, quarter), BF16),
        vmem((SPLIT * per, width), BF16),
        vmem((SPLIT * per, units), BF16),
        vmem((FOLD, SPLIT, per, quarter), BF16),
        vmem((FOLD, SPLIT, per, quarter), BF16),
        vmem((win, 16, quarter), BF16),
        vmem((win, 16, quarter), BF16),
        vmem((SPLIT * per, lanes), F32),
        vmem((SPLIT, win, 8, lanes), F32),
        vmem((SPLIT, rows, lanes), F32),
        vmem((SPLIT, rows, lanes), F32),
        vmem((rows, rows_tok), F32),
        vmem((rows_tok, width), BF16),
        sems((7,)),
        sems((FOLD,)),
        *[sems((win,))] * 4,
        *[sems((win, SPLIT))] * 2,
        *[sems((FOLD, SPLIT))] * 2,
        *[sems((win,))] * 2,
        *[sems((SPLIT, win))] * 2,
    ]
    return pl.pallas_call(
        functools.partial(kernel, n, local),
        out_shape=jax.ShapeDtypeStruct((rows_tok, width), BF16),
        in_specs=[pl.BlockSpec(memory_space=pl.ANY)] * 7,
        out_specs=pl.BlockSpec(memory_space=pl.ANY),
        scratch_shapes=scratch,
        compiler_params=pltpu.CompilerParams(
            collective_id=0, has_side_effects=True, vmem_limit_bytes=48 * 1024 * 1024
        ),
    )(tokens, expert_ids, lengths, router, w_gate, w_up, w_down)


def solution(mesh):
    placed = (
        P(("groups", "expert"), None),
        P(("groups", "expert"), None),
        P("groups"),
        P("expert", None),
        P("expert", None, None),
        P("expert", None, None),
        P("expert", None, None),
    )
    return jax.shard_map(
        shards, mesh=mesh, in_specs=placed, out_specs=P(("groups", "expert"), None), check_vma=False
    )
```

time: 115 us -> 40.6 us (0.35)
  waiting for transfers between devices: 41.3 us -> 0 us
  Pallas kernels: 0 us -> 33.9 us
  blocking collectives: 33.4 us -> 0 us
  between operations: 14.2 us -> 0.67 us
  matrix products: 12.4 us -> 0 us
  local copies, waits for them, and re-layouts: 11.3 us -> 5.82 us
  other arithmetic: 2.48 us -> 0 us
    all_gather x1 -> x0, waiting for transfers between devices: 40.6 us -> none  [shards(): lax.all_gather(router, 'expert', axis=0, tiled=True)]
    pallas_call x0 -> x1, Pallas kernels: none -> 33.9 us  [shards(): pl.pallas_call(functools.partial(kernel, n, local), out_shape=jax.ShapeDt...]
    all_to_all x2 -> x0, blocking collectives: 33.4 us -> none  [the longest x1 16.9 us: shards(): lax.all_to_all(partials, 'expert', split_axis=0, concat_axis=0, tiled=True)]
    dot_general x5 -> x0, matrix products: 12.4 us -> none  [the longest x1 4.62 us: shards(): jnp.dot(hidden, w_down[0], preferred_element_type=jnp.float32)]
    gather x5 -> x0, local copies, waits for them, and re-layouts: 8.91 us -> none  [shards(): picked = jnp.take_along_axis(scores, expert_ids, axis=1)]
    unnamed x5 -> x8, local copies, waits for them, and re-layouts: 0.8 us -> 5.82 us
    another operation x2 -> x0, other arithmetic: 1.33 us -> none
  transfers between devices with their start and end apart: 1 -> 0, of which waited for: 1 -> 0; matrix products, arithmetic and copies ran while one was open for 4% -> 0% of each run, Pallas kernels for 0% -> 0%
where the time goes in v1:
time: 40.6 us; the launch traced here: 40.4 us
  Pallas kernels  33.9 us (83%)
  local copies, waits for them, and re-layouts  5.82 us (14%)
  between operations  0.67 us (2%)
    pallas_call x1, Pallas kernels, shards(): pl.pallas_call(functools.partial(kernel, n, local), out_shape=jax.ShapeDt...  33.9 us
    unnamed x8, local copies, waits for them, and re-layouts  5.82 us

profile of v1, /device:TPU:0, one launch (start us, length us, event | category | flops | bytes accessed | tf_op | source)
XLA Modules:
  0.0 40.4 jit_solution(924984217711695089)
XLA Ops:
  0.7 0.8 %copy.8.ids_hbm = s32[128,8]{1,0:T(8,128)S(1)} copy(s32[128,8]{0,1:T(8,128)} %param.8) | data formatting | bytes 8192 | tf_op args[1]
  1.4 0.0 copy-start
  1.4 2.0 %copy-done = bf16[1,3584,512]{2,1,0:T(8,128)(2,1)S(1)} copy-done((bf16[1,3584,512]{2,1,0:T(8,128)(2,1)S(1)}, bf16[1,3584,512]{2,1,0:T(8,128)(2,1)}, u32[]{:S(2)}) %copy-start) | copy-done | bytes 3670040
  3.5 0.0 copy-start.1
  3.5 1.2 %copy-done.1 = bf16[128,3584]{1,0:T(8,128)(2,1)S(1)} copy-done((bf16[128,3584]{1,0:T(8,128)(2,1)S(1)}, bf16[128,3584]{1,0:T(8,128)(2,1)}, u32[]{:S(2)}) %copy-start.1) | copy-done | bytes 917528
  4.7 0.0 copy-start.2
  4.7 0.9 %copy-done.2 = bf16[16,3584]{1,0:T(8,128)(2,1)S(1)} copy-done((bf16[16,3584]{1,0:T(8,128)(2,1)S(1)}, bf16[16,3584]{1,0:T(8,128)(2,1)}, u32[]{:S(2)}) %copy-start.2) | copy-done | bytes 114712
  5.6 33.9 %shard_map.73 = bf16[128,3584]{1,0:T(8,128)(2,1)S(1)} custom-call(bf16[128,3584]{1,0:T(8,128)(2,1)S(1)} %copy-done.1, s32[128,8]{1,0:T(8,128)S(1)} %copy.8.ids_hbm, s32[1]{0:T(128)S(6)} %copy.10.len_hbm, bf16[16,3584]{1,0:T(8,128)(2,1)S(1)} %copy-done.2, bf16[1,3584,512]{2,1,0:T(8,128)(2,1)S(1)} %copy-done, bf16[1,3584,512]{2,1,0:T(8,128)(2,1)} %up_hbm.1, ...), custom_call_target="tpu_custom_call" | custom-call | tf_op jit(solution)/shard_map/pallas_call | solution.py:302
  39.4 0.9 %copy.11 = bf16[128,3584]{1,0:T(8,128)(2,1)} copy(bf16[128,3584]{1,0:T(8,128)(2,1)S(1)} %shard_map.73) | data formatting | bytes 1835008
Async XLA Ops:
  1.4 2.0 %copy-start = (bf16[1,3584,512]{2,1,0:T(8,128)(2,1)S(1)}, bf16[1,3584,512]{2,1,0:T(8,128)(2,1)}, u32[]{:S(2)}) copy-start(bf16[1,3584,512]{2,1,0:T(8,128)(2,1)} %gate_hbm.1) | copy-start | bytes 11010052
  3.5 1.2 %copy-start.1 = (bf16[128,3584]{1,0:T(8,128)(2,1)S(1)}, bf16[128,3584]{1,0:T(8,128)(2,1)}, u32[]{:S(2)}) copy-start(bf16[128,3584]{1,0:T(8,128)(2,1)} %tokens_hbm.1) | copy-start | bytes 2752516
  4.7 0.9 %copy-start.2 = (bf16[16,3584]{1,0:T(8,128)(2,1)S(1)}, bf16[16,3584]{1,0:T(8,128)(2,1)}, u32[]{:S(2)}) copy-start(bf16[16,3584]{1,0:T(8,128)(2,1)} %router_hbm.1) | copy-start | bytes 344068

commit v2 on v1

--- a/solution.py
+++ b/solution.py
@@ -31,10 +31,10 @@
 
 
 def kernel(
-    n, local, tokens_hbm, ids_hbm, len_hbm, router_hbm, gate_hbm, up_hbm, down_hbm, out_hbm,
+    n, local, tokens_hbm, ids_hbm, len_hbm, router_hbm, gate_hbm, up_hbm, down_hbm, out,
     tok, ids, length, wg, wu, wd, routed, fold_out, fold_in, x, hidden, part, reduced, back_out, back,
-    logit, logits, mask, num_mask, onehot, out,
-    load_sem, out_sem, disp_s, disp_r, rout_s, rout_r, fwd_s, fwd_r, red_s, red_r, back_s, back_r, log_s, log_r,
+    logit, logits, mask, num_mask, onehot,
+    load_sem, disp_s, disp_r, rout_s, rout_r, fwd_s, fwd_r, red_s, red_r, back_s, back_r, log_s, log_r,
 ):
     win = n // SPLIT
     rows = win * 16
@@ -77,9 +77,8 @@
 
     loads[0].wait()
     loads[1].wait()
-    ids_b = ids[...].astype(F32).astype(BF16)
-    eye = (iota((8, 8), 0) == iota((8, 8), 1)).astype(F32).astype(BF16)
-    ids_t = dot_nt(eye, ids_b).astype(jnp.int32)
+    ids_t = ids[...]
+    ids_b = ids_t.astype(F32).astype(BF16)
     first = me * rows_tok
     alive = mod(first, SEQ_LEN) + iota((rows, rows_tok), 1) < length[lax.div(first, jnp.int32(SEQ_LEN))]
     row = iota((rows, rows_tok), 0)
@@ -130,7 +129,7 @@
             )
             fwd[dw, dr].start()
 
-    slot_ids = dot(hot.astype(BF16), ids_b)
+    slot_ids = dot_nt(hot.astype(BF16), ids_b)
     srow = iota((rows, lanes), 0)
     lane = iota((rows, lanes), 1)
     slot_dw = lax.div(srow, jnp.int32(16))
@@ -143,7 +142,7 @@
         which = jnp.where(good, chunk * local + lane_e, -1)
         as_float = which.astype(F32)
         hit = jnp.zeros((rows, lanes), F32)
-        for k in range(ids_b.shape[1]):
+        for k in range(ids_b.shape[0]):
             hit = jnp.where(as_float == slot_ids[:, k : k + 1], 1.0, hit)
         mask[i] = hit
         num_mask[i] = jnp.where(which == mine, 1.0, 0.0)
@@ -238,21 +237,16 @@
     for dw in range(1, win):
         backs[dw].wait_recv()
     returned = back[...].reshape(rows, quarter)
-    stores = []
     for q in range(FOLD):
         cols = slice(q * quarter, (q + 1) * quarter)
         acc = jnp.zeros((rows_tok, quarter), F32)
         for piece in (high, middle, low):
             acc = acc + dot(jnp.where(ccol == q, piece, 0.0).astype(BF16), returned)
         out[:, cols] = acc.astype(BF16)
-        stores.append(pltpu.make_async_copy(out.at[:, cols], out_hbm.at[:, cols], out_sem.at[q]))
-        stores[q].start()
 
     for copies in (disp[1:], rout[1:], backs[1:], fwd.values(), red.values(), logs.values()):
         for copy in copies:
             copy.wait_send()
-    for store in stores:
-        store.wait()
 
 
 def shards(tokens, expert_ids, lengths, router, w_gate, w_up, w_down):
@@ -271,7 +265,7 @@
     sems = pltpu.SemaphoreType.DMA
     scratch = [
         vmem((rows_tok, width), BF16),
-        vmem(expert_ids.shape, jnp.int32),
+        vmem(expert_ids.shape[::-1], jnp.int32),
         pltpu.SMEM(lengths.shape, jnp.int32),
         vmem((width, units), BF16),
         vmem((width, units), BF16),
@@ -290,9 +284,7 @@
         vmem((SPLIT, rows, lanes), F32),
         vmem((SPLIT, rows, lanes), F32),
         vmem((rows, rows_tok), F32),
-        vmem((rows_tok, width), BF16),
         sems((7,)),
-        sems((FOLD,)),
         *[sems((win,))] * 4,
         *[sems((win, SPLIT))] * 2,
         *[sems((FOLD, SPLIT))] * 2,
@@ -302,13 +294,13 @@
     return pl.pallas_call(
         functools.partial(kernel, n, local),
         out_shape=jax.ShapeDtypeStruct((rows_tok, width), BF16),
-        in_specs=[pl.BlockSpec(memory_space=pl.ANY)] * 7,
-        out_specs=pl.BlockSpec(memory_space=pl.ANY),
+        in_specs=[pl.BlockSpec(memory_space=pltpu.HBM)] * 7,
+        out_specs=pl.BlockSpec(memory_space=pltpu.VMEM),
         scratch_shapes=scratch,
         compiler_params=pltpu.CompilerParams(
-            collective_id=0, has_side_effects=True, vmem_limit_bytes=48 * 1024 * 1024
+            collective_id=0, has_side_effects=True, vmem_limit_bytes=56 * 1024 * 1024
         ),
-    )(tokens, expert_ids, lengths, router, w_gate, w_up, w_down)
+    )(tokens, expert_ids.T, lengths, router, w_gate, w_up, w_down)
 
 
 def solution(mesh):

time: 40.6 us -> 36.2 us (0.89)
  local copies, waits for them, and re-layouts: 5.82 us -> 2.16 us
  Pallas kernels: 33.9 us -> 33.2 us
    unnamed x8 -> x1, local copies, waits for them, and re-layouts: 5.82 us -> 2.16 us
    pallas_call x1, Pallas kernels: 33.9 us -> 33.2 us  [shards(): pl.pallas_call(functools.partial(kernel, n, local), out_shape=jax.ShapeDt...]
where the time goes in v2:
time: 36.2 us; the launch traced here: 36 us
  Pallas kernels  33.2 us (92%)
  local copies, waits for them, and re-layouts  2.16 us (6%)
  between operations  0.66 us (2%)
    pallas_call x1, Pallas kernels, shards(): pl.pallas_call(functools.partial(kernel, n, local), out_shape=jax.ShapeDt...  33.2 us
    unnamed x1, local copies, waits for them, and re-layouts  2.16 us

profile of v2, /device:TPU:0, one launch (start us, length us, event | category | flops | bytes accessed | tf_op | source)
XLA Modules:
  0.0 36.0 jit_solution(8178861662892810311)
XLA Ops:
  0.7 33.2 %shard_map.73 = bf16[128,3584]{1,0:T(8,128)(2,1)} custom-call(bf16[128,3584]{1,0:T(8,128)(2,1)} %tokens_hbm.1, s32[8,128]{1,0:T(8,128)} %bitcast.1, s32[1]{0:T(128)S(6)} %copy.9.len_hbm, bf16[16,3584]{1,0:T(8,128)(2,1)} %router_hbm.1, bf16[1,3584,512]{2,1,0:T(8,128)(2,1)} %gate_hbm.1, bf16[1,3584,512]{2,1,0:T(8,128)(2,1)} %up_hbm.1, ...), custom_call_target="tpu_custom_call" | custom-call | tf_op jit(solution)/shard_map/pallas_call | solution.py:294
  33.9 2.2 %copy.10 = bf16[128,3584]{1,0:T(8,128)(2,1)} copy(bf16[128,3584]{1,0:T(8,128)(2,1)} %shard_map.73) | data formatting | bytes 1835008

commit v3 on v2

--- a/solution.py
+++ b/solution.py
@@ -47,8 +47,17 @@
     w = lax.div(me, jnp.int32(SPLIT))
     r = me - w * SPLIT
 
-    def other(dw, dr):
-        return {"expert": mod(w + (dw + win), win) * SPLIT + mod(r + (dr + SPLIT), SPLIT)}
+    def flip(at, bit):
+        return at + bit - 2 * bit * mod(lax.div(at, jnp.int32(bit)), 2)
+
+    def place_of(i):
+        at = r
+        for bit in (1, 2):
+            at = flip(at, bit) if i & bit else at
+        return at
+
+    def other(dw, i):
+        return {"expert": mod(w + (dw + win), win) * SPLIT + place_of(i)}
 
     loads = [
         pltpu.make_async_copy(src, dst, load_sem.at[i])
@@ -110,24 +119,36 @@
         disp.append(send(fold_out.at[dw], fold_in.at[0, dw], disp_s.at[dw], disp_r.at[dw], other(dw, 0)))
         disp[dw].start()
     fwd = {}
-    for dr in range(1, SPLIT):
-        fwd[0, dr] = send(
-            fold_in.at[0, 0], fold_in.at[dr, 0], fwd_s.at[0, dr], fwd_r.at[0, dr], other(0, dr)
-        )
-        fwd[0, dr].start()
+
+    def forward(src, dst, dw, i):
+        fwd[dw, dst] = send(
+            fold_in.at[src, dw], fold_in.at[dst, dw], fwd_s.at[dw, dst], fwd_r.at[dw, dst], other(0, i)
+        )
+        fwd[dw, dst].start()
+
+    for dw in range(win):
+        if dw:
+            disp[dw].wait_recv()
+        forward(0, 2, dw, 2)
+        forward(0, 1, dw, 1)
+
     loads[3].wait()
-    rout = [None]
-    for dw in range(1, win):
-        rout.append(send(routed.at[0], routed.at[dw], rout_s.at[dw], rout_r.at[dw], other(dw, 0)))
-        rout[dw].start()
-
-    for dw in range(1, win):
-        disp[dw].wait_recv()
-        for dr in range(1, SPLIT):
-            fwd[dw, dr] = send(
-                fold_in.at[0, dw], fold_in.at[dr, dw], fwd_s.at[dw, dr], fwd_r.at[dw, dr], other(0, dr)
+    rout, arrived = {}, set()
+
+    def push(held):
+        bit = (held & -held or win) // 2
+        while bit:
+            rout[held + bit] = send(
+                routed.at[held], routed.at[held + bit], rout_s.at[held + bit], rout_r.at[held + bit],
+                {"expert": flip(w, bit) * SPLIT + r},
             )
-            fwd[dw, dr].start()
+            rout[held + bit].start()
+            bit //= 2
+
+    def low_bit(d):
+        return d & -d
+
+    push(0)
 
     slot_ids = dot_nt(hot.astype(BF16), ids_b)
     srow = iota((rows, lanes), 0)
@@ -138,7 +159,7 @@
     good = (lane_dw < win) & (lane_e < local)
     mine = mod(w + slot_dw, win)
     for i in range(SPLIT):
-        chunk = mod(w + slot_dw - lane_dw + 2 * win, win) * SPLIT + mod(r + i, SPLIT)
+        chunk = (mine ^ lane_dw) * SPLIT + place_of(i)
         which = jnp.where(good, chunk * local + lane_e, -1)
         as_float = which.astype(F32)
         hit = jnp.zeros((rows, lanes), F32)
@@ -150,8 +171,11 @@
     prow, pcol = iota((rows, rows), 0), iota((rows, rows), 1)
     q_of, dw_of, c_of = lax.div(prow, jnp.int32(per)), lax.div(mod(prow, per), jnp.int32(CAP)), mod(prow, CAP)
     perm = (pcol == dw_of * 16 + q_of * CAP + c_of).astype(F32).astype(BF16)
+    for dw in range(win):
+        fwd[dw, 2].wait_recv()
+        forward(2, 3, dw, 1)
     for i in range(SPLIT):
-        if i:
+        if i in (1, 3):
             for dw in range(win):
                 fwd[dw, i].wait_recv()
         plain = dot(perm, fold_in[i].reshape(rows, quarter)).astype(BF16)
@@ -167,20 +191,32 @@
         g = dot(x[...], wg[:, cols])
         u = dot(x[...], wu[:, cols])
         hidden[:, cols] = (g * jax.nn.sigmoid(g) * u).astype(BF16)
+    for held in sorted(range(1, win), key=lambda d: (-low_bit(d), d)):
+        if low_bit(held) > 1:
+            rout[held].wait_recv()
+            arrived.add(held)
+            push(held)
     loads[6].wait()
     red = {}
+
+    def give(q, src, dst, i):
+        red[q, dst] = send(part.at[q, src], reduced.at[q, dst], red_s.at[q, dst], red_r.at[q, dst], other(0, i))
+        red[q, dst].start()
+
     for q in range(FOLD):
         part[q] = dot(hidden[...], wd[:, q * quarter : (q + 1) * quarter]).astype(BF16).reshape(
             SPLIT, per, quarter
         )
-        for i in range(1, SPLIT):
-            red[q, i] = send(
-                part.at[q, i], reduced.at[q, i], red_s.at[q, i], red_r.at[q, i], other(0, -i)
-            )
-            red[q, i].start()
-
-    for dw in range(1, win):
-        rout[dw].wait_recv()
+        give(q, 3, 3, 1)
+        give(q, 1, 1, 1)
+    for q in range(FOLD):
+        red[q, 3].wait_recv()
+        part[q, 2] = (part[q, 2].astype(F32) + reduced[q, 3].astype(F32)).astype(BF16)
+        give(q, 2, 2, 2)
+
+    for held in range(1, win):
+        if held not in arrived:
+            rout[held].wait_recv()
     logit[...] = jnp.zeros_like(logit)
     logit[:, : win * epad] = dot_nt(x[...], routed[...].reshape(win * epad, width))
     logs = {}
@@ -188,7 +224,7 @@
         for dw in range(win):
             src = logit.at[pl.ds(i * per + dw // 2 * 8, 8)]
             if i or dw:
-                logs[i, dw] = send(src, logits.at[i, dw], log_s.at[i, dw], log_r.at[i, dw], other(-dw, -i))
+                logs[i, dw] = send(src, logits.at[i, dw], log_s.at[i, dw], log_r.at[i, dw], other(-dw, i))
                 logs[i, dw].start()
             else:
                 logits[0, 0] = logit[:8]
@@ -198,7 +234,7 @@
     total = jnp.zeros((rows, quarter), F32)
     for q in range(FOLD):
         summed = part[q, 0].astype(F32)
-        for i in range(1, SPLIT):
+        for i in (1, 2):
             red[q, i].wait_recv()
             summed = summed + reduced[q, i].astype(F32)
         spread = ((fcol == place) & (mod(lax.div(frow, jnp.int32(CAP)), FOLD) == q)).astype(F32).astype(BF16)
@@ -244,7 +280,7 @@
             acc = acc + dot(jnp.where(ccol == q, piece, 0.0).astype(BF16), returned)
         out[:, cols] = acc.astype(BF16)
 
-    for copies in (disp[1:], rout[1:], backs[1:], fwd.values(), red.values(), logs.values()):
+    for copies in (disp[1:], rout.values(), backs[1:], fwd.values(), red.values(), logs.values()):
         for copy in copies:
             copy.wait_send()
 

time: 36.2 us -> 32.9 us (0.909)
  Pallas kernels: 33.2 us -> 29.9 us
    pallas_call x1, Pallas kernels: 33.2 us -> 29.9 us  [shards(): pl.pallas_call(functools.partial(kernel, n, local), out_shape=jax.ShapeDt...]
where the time goes in v3:
time: 32.9 us; the launch traced here: 32.7 us
  Pallas kernels  29.9 us (91%)
  local copies, waits for them, and re-layouts  2.16 us (7%)
  between operations  0.66 us (2%)
    pallas_call x1, Pallas kernels, shards(): pl.pallas_call(functools.partial(kernel, n, local), out_shape=jax.ShapeDt...  29.9 us
    unnamed x1, local copies, waits for them, and re-layouts  2.16 us

profile of v3, /device:TPU:0, one launch (start us, length us, event | category | flops | bytes accessed | tf_op | source)
XLA Modules:
  0.0 32.7 jit_solution(12157721214708097734)
XLA Ops:
  0.7 29.9 %shard_map.73 = bf16[128,3584]{1,0:T(8,128)(2,1)} custom-call(bf16[128,3584]{1,0:T(8,128)(2,1)} %tokens_hbm.1, s32[8,128]{1,0:T(8,128)} %bitcast.1, s32[1]{0:T(128)S(6)} %copy.9.len_hbm, bf16[16,3584]{1,0:T(8,128)(2,1)} %router_hbm.1, bf16[1,3584,512]{2,1,0:T(8,128)(2,1)} %gate_hbm.1, bf16[1,3584,512]{2,1,0:T(8,128)(2,1)} %up_hbm.1, ...), custom_call_target="tpu_custom_call" | custom-call | tf_op jit(solution)/shard_map/pallas_call | solution.py:330
  30.6 2.2 %copy.10 = bf16[128,3584]{1,0:T(8,128)(2,1)} copy(bf16[128,3584]{1,0:T(8,128)(2,1)} %shard_map.73) | data formatting | bytes 1835008

commit v4 on v3

--- a/solution.py
+++ b/solution.py
@@ -31,9 +31,9 @@
 
 
 def kernel(
-    n, local, tokens_hbm, ids_hbm, len_hbm, router_hbm, gate_hbm, up_hbm, down_hbm, out,
-    tok, ids, length, wg, wu, wd, routed, fold_out, fold_in, x, hidden, part, reduced, back_out, back,
-    logit, logits, mask, num_mask, onehot,
+    n, local, tokens_hbm, ids_hbm, len_hbm, router_hbm, gate_hbm, up_hbm, down_hbm, comb_out, back_hbm,
+    tok, ids, length, wg, wu, wd, routed, fold_out, fold_in, x, hidden, part, reduced, back_out,
+    logit, logits, mask, num_mask, onehot, back,
     load_sem, disp_s, disp_r, rout_s, rout_r, fwd_s, fwd_r, red_s, red_r, back_s, back_r, log_s, log_r,
 ):
     win = n // SPLIT
@@ -265,24 +265,28 @@
     filled = jnp.sum(hot, axis=1, keepdims=True) > 0.5
     weight = jnp.where(filled, 2.5 * num / jnp.where(filled, den, 1.0), 0.0)
     combine = (hot * weight).T
+    comb_out[...] = combine
+    for dw in range(1, win):
+        backs[dw].wait_recv()
+    back_hbm[...] = back[...]
+
+    for copies in (disp[1:], rout.values(), backs[1:], fwd.values(), red.values(), logs.values()):
+        for copy in copies:
+            copy.wait_send()
+
+
+def mix(combine_ref, returned_ref, out_ref):
+    combine = combine_ref[...]
+    rows_tok, rows = combine.shape
     high = combine.astype(BF16).astype(F32)
     middle = (combine - high).astype(BF16).astype(F32)
     low = combine - high - middle
-    ccol = mod(lax.div(iota((rows_tok, rows), 1), jnp.int32(CAP)), FOLD)
-
-    for dw in range(1, win):
-        backs[dw].wait_recv()
-    returned = back[...].reshape(rows, quarter)
-    for q in range(FOLD):
-        cols = slice(q * quarter, (q + 1) * quarter)
-        acc = jnp.zeros((rows_tok, quarter), F32)
-        for piece in (high, middle, low):
-            acc = acc + dot(jnp.where(ccol == q, piece, 0.0).astype(BF16), returned)
-        out[:, cols] = acc.astype(BF16)
-
-    for copies in (disp[1:], rout.values(), backs[1:], fwd.values(), red.values(), logs.values()):
-        for copy in copies:
-            copy.wait_send()
+    returned = returned_ref[...].reshape(rows, returned_ref.shape[2])
+    turn = mod(lax.div(iota((rows_tok, rows), 1), jnp.int32(CAP)), FOLD)
+    acc = jnp.zeros(out_ref.shape, F32)
+    for piece in (high, middle, low):
+        acc = acc + dot(jnp.where(turn == pl.program_id(0), piece, 0.0).astype(BF16), returned)
+    out_ref[...] = acc.astype(BF16)
 
 
 def shards(tokens, expert_ids, lengths, router, w_gate, w_up, w_down):
@@ -314,12 +318,12 @@
         vmem((FOLD, SPLIT, per, quarter), BF16),
         vmem((FOLD, SPLIT, per, quarter), BF16),
         vmem((win, 16, quarter), BF16),
-        vmem((win, 16, quarter), BF16),
         vmem((SPLIT * per, lanes), F32),
         vmem((SPLIT, win, 8, lanes), F32),
         vmem((SPLIT, rows, lanes), F32),
         vmem((SPLIT, rows, lanes), F32),
         vmem((rows, rows_tok), F32),
+        vmem((win, 16, quarter), BF16),
         sems((7,)),
         *[sems((win,))] * 4,
         *[sems((win, SPLIT))] * 2,
@@ -327,16 +331,27 @@
         *[sems((win,))] * 2,
         *[sems((SPLIT, win))] * 2,
     ]
-    return pl.pallas_call(
+    combine, returned = pl.pallas_call(
         functools.partial(kernel, n, local),
-        out_shape=jax.ShapeDtypeStruct((rows_tok, width), BF16),
+        out_shape=(
+            jax.ShapeDtypeStruct((rows_tok, rows), F32),
+            jax.ShapeDtypeStruct((win, 16, quarter), BF16),
+        ),
         in_specs=[pl.BlockSpec(memory_space=pltpu.HBM)] * 7,
-        out_specs=pl.BlockSpec(memory_space=pltpu.VMEM),
+        out_specs=[pl.BlockSpec(memory_space=pltpu.VMEM)] * 2,
         scratch_shapes=scratch,
         compiler_params=pltpu.CompilerParams(
             collective_id=0, has_side_effects=True, vmem_limit_bytes=56 * 1024 * 1024
         ),
     )(tokens, expert_ids.T, lengths, router, w_gate, w_up, w_down)
+    whole = pl.BlockSpec((rows_tok, rows), lambda q: (0, 0))
+    return pl.pallas_call(
+        mix,
+        grid=(FOLD,),
+        out_shape=jax.ShapeDtypeStruct((rows_tok, width), BF16),
+        in_specs=[whole, pl.BlockSpec((win, 16, quarter), lambda q: (0, 0, 0))],
+        out_specs=pl.BlockSpec((rows_tok, quarter), lambda q: (0, q)),
+    )(combine, returned)
 
 
 def solution(mesh):

time: 32.9 us -> 32.9 us (level)
  local copies, waits for them, and re-layouts: 2.16 us -> 0 us
  Pallas kernels: 29.9 us -> 32 us
    unnamed x1 -> x0, local copies, waits for them, and re-layouts: 2.16 us -> none
    pallas_call x1 -> x2, Pallas kernels: 29.9 us -> 32 us  [the longest x1 28.7 us: shards(): pl.pallas_call(functools.partial(kernel, n, local), out_shape=(jax.ShapeD...]
where the time goes in v4:
time: 32.9 us; the launch traced here: 32.7 us
  Pallas kernels  32 us (97%)
  between operations  0.66 us (2%)
    pallas_call x1, Pallas kernels, shards(): pl.pallas_call(functools.partial(kernel, n, local), out_shape=(jax.ShapeD...  28.7 us
    pallas_call x1, Pallas kernels, shards(): pl.pallas_call(mix, grid=(FOLD,), out_shape=jax.ShapeDtypeStruct((rows_to...  3.32 us

profile of v4, /device:TPU:0, one launch (start us, length us, event | category | flops | bytes accessed | tf_op | source)
XLA Modules:
  0.0 32.7 jit_solution(5448157676885755534)
XLA Ops:
  0.7 28.7 %shard_map.73 = (f32[128,64]{1,0:T(8,128)}, bf16[4,16,896]{2,1,0:T(8,128)(2,1)}) custom-call(bf16[128,3584]{1,0:T(8,128)(2,1)} %tokens_hbm.1, s32[8,128]{1,0:T(8,128)} %bitcast.1, s32[1]{0:T(128)S(6)} %copy.8.len_hbm, bf16[16,3584]{1,0:T(8,128)(2,1)} %router_hbm.1, bf16[1,3584,512]{2,1,0:T(8,128)(2,1)} %gate_hbm.1, bf16[1,3584,512]{2,1,0:T(8,128)(2,1)} %up_hbm.1, ...), custom_call_target="tpu_custom_call" | custom-call | tf_op jit(solution)/shard_map/pallas_call | solution.py:334
  29.4 3.3 %shard_map.74 = bf16[128,3584]{1,0:T(8,128)(2,1)} custom-call(f32[128,64]{1,0:T(8,128)} %get-tuple-element.7.combine_ref, bf16[4,16,896]{2,1,0:T(8,128)(2,1)} %get-tuple-element.8.returned_ref), custom_call_target="tpu_custom_call" | custom-call | tf_op jit(solution)/shard_map/pallas_call | solution.py:348
